TPU v7x, 128 devices: a whole 4x4x4 slice. The times are simulated.
128 devices in a mesh: row: 4 (over y), col: 4 (over x_lo, core), depth: 8 (over x_hi, z).
Axes of the slice: x: 4 (x_hi: 2, x_lo: 2; x = x_hi * 2 + x_lo), y: 4, z: 4, core: 2. Of those that a mesh axis runs over, the one named last changes fastest.
Arguments:
- inputs: bfloat16 [2048, 12288], P('col', ('row', 'depth')), may hold values from -0.23925781 to 0.23925781
- weight_in: bfloat16 [12288, 24576], P(('row', 'depth'), 'col'), may hold values from -0.0546875 to 0.0546875
- saved_pre: bfloat16 [2048, 24576], P(('row', 'depth'), 'col'), may hold values from -10 to 10
- grad_hidden: bfloat16 [2048, 24576], P(('row', 'depth'), 'col'), may hold values from -6 to 6
Outputs:
- grad_inputs: bfloat16 [2048, 12288], P('col', ('row', 'depth'))
- grad_weight: bfloat16 [12288, 24576], P(('row', 'depth'), 'col')
All inputs are finite; a program needn't handle non-finite values.
Results may differ from a plain program's by a relative error of at most 0.0049.
Values may be sent and summed in bfloat16 or wider, within the bound.
A program may use at most 192 MiB of HBM per device.

v0:
```python
import jax
import jax.numpy as jnp
from jax import lax
from jax.sharding import PartitionSpec as P


def gelu_back(grad_hidden, saved_pre):
    pre = saved_pre.astype(jnp.float32)
    value, pull = jax.vjp(lambda a: jax.nn.gelu(a, approximate=True), pre)
    return pull(grad_hidden.astype(jnp.float32))[0].astype(jnp.bfloat16)


def local(inputs, weight_in, saved_pre, grad_hidden):
    all_inputs = lax.all_gather(inputs, "col", axis=0, tiled=True)
    local_grad = gelu_back(grad_hidden, saved_pre)
    grad_pre = lax.all_gather(local_grad, ("row", "depth"), axis=0, tiled=True)
    weight_sum = lax.dot_general(
        all_inputs, grad_pre, (((0,), (0,)), ((), ())), preferred_element_type=jnp.float32
    )
    partial_inputs = lax.dot_general(
        grad_pre, weight_in, (((1,), (1,)), ((), ())), preferred_element_type=jnp.float32
    )
    grad_inputs = lax.psum_scatter(partial_inputs, "col", scatter_dimension=0, tiled=True).astype(
        jnp.bfloat16
    )
    return (grad_inputs, weight_sum.astype(jnp.bfloat16))


def solution(mesh):
    return jax.shard_map(
        local,
        mesh=mesh,
        in_specs=(
            P("col", ("row", "depth")),
            P(("row", "depth"), "col"),
            P(("row", "depth"), "col"),
            P(("row", "depth"), "col"),
        ),
        out_specs=(P("col", ("row", "depth")), P(("row", "depth"), "col")),
        check_vma=False,
    )
```

profile of v0, /device:TPU:1, one launch (start us, length us, event | category | flops | bytes accessed | tf_op | source)
XLA Modules:
  0.0 297.9 jit_solution(7049917879169984197)
XLA Ops:
  7.2 0.0 all-gather.3.cloned.1.call-start
  7.2 3.4 %fusion.4 = bf16[64,6144]{1,0:T(8,128)(2,1)} fusion(bf16[64,6144]{1,0:T(8,128)(2,1)} %param.7, bf16[64,6144]{1,0:T(8,128)(2,1)} %param.6), kind=kLoop, calls=%fused_computation.10 | loop fusion | flops 8650752 | bytes 2359296 | tf_op jit(solution)/shard_map/convert_element_type | solution.py:10
  10.6 0.0 all-gather.3.cloned.1.call-update
  10.6 0.0 all-gather.5.cloned.1.call-start
  10.7 0.7 all-gather.5.cloned.1.call-update
  11.4 0.0 reduce-scatter.2.cloned.1.call-start
  11.4 212.7 %all-gather.3.cloned.1.call-done = bf16[2048,6144]{1,0:T(8,128)(2,1)} async-done(((bf16[64,6144]{1,0:T(8,128)(2,1)}), bf16[2048,6144]{1,0:T(8,128)(2,1)}) %all-gather.3.cloned.1.call-update) | async-done | bytes 25165840 | tf_op jit(solution)/shard_map/all_gather | solution.py:16
  224.2 19.4 %fusion.11 = f32[2048,384]{1,0:T(8,128)} fusion(bf16[2048,6144]{1,0:T(8,128)(2,1)} %all-gather.3.cloned.1.call-done, bf16[384,6144]{1,0:T(8,128)(2,1)} %param.5), kind=kOutput, calls=%fused_computation.17 | convolution fusion | flops 9663676416 | bytes 33030144 | tf_op jit(solution)/shard_map/dot_general | solution.py:20
  243.5 0.0 reduce-scatter.2.cloned.1.call-update
  243.5 5.9 %all-gather.5.cloned.1.call-done = bf16[2048,384]{1,0:T(8,128)(2,1)} async-done(((bf16[512,384]{1,0:T(8,128)(2,1)}), bf16[2048,384]{1,0:T(8,128)(2,1)}) %all-gather.5.cloned.1.call-update) | async-done | bytes 1572880 | tf_op jit(solution)/shard_map/all_gather | solution.py:14
  249.4 19.9 %fusion = bf16[384,6144]{0,1:T(8,128)(2,1)} fusion(bf16[2048,6144]{1,0:T(8,128)(2,1)} %all-gather.3.cloned.1.call-done, bf16[2048,384]{1,0:T(8,128)(2,1)} %all-gather.5.cloned.1.call-done), kind=kOutput, calls=%fused_computation.1 | convolution fusion | flops 9666035712 | bytes 31457280 | tf_op jit(solution)/shard_map/dot_general | solution.py:17
  269.4 6.6 %copy.6 = bf16[384,6144]{1,0:T(8,128)(2,1)} copy(bf16[384,6144]{0,1:T(8,128)(2,1)} %fusion) | data formatting | bytes 9437184
  276.0 13.4 %reduce-scatter.2.cloned.1.call-done = f32[512,384]{1,0:T(8,128)} async-done(((f32[2048,384]{1,0:T(8,128)}), f32[512,384]{1,0:T(8,128)}) %reduce-scatter.2.cloned.1.call-update) | async-done | bytes 786448 | tf_op jit(solution)/shard_map/reduce_scatter | solution.py:23
  289.4 1.9 convert_element_type.21
Async XLA Ops:
  7.2 217.0 %all-gather.3.cloned.1.call-start = ((), (), s32[]{:S(2)}) async-start(), calls=%async_computation.1 | async-start | bytes 25952256 | tf_op jit(solution)/shard_map/all_gather | solution.py:16
  10.6 238.8 %all-gather.5.cloned.1.call-start = ((), (), s32[]{:S(2)}) async-start(), calls=%async_computation.3 | async-start | bytes 1966080 | tf_op jit(solution)/shard_map/all_gather | solution.py:14
  11.4 278.0 %reduce-scatter.2.cloned.1.call-start = ((), (), s32[]{:S(2)}) async-start(), calls=%async_computation.2 | async-start | bytes 3932160 | tf_op jit(solution)/shard_map/reduce_scatter | solution.py:23
Sparse Core Ops, SparseCore 0:
  11.7 212.4 all-gather.2
  225.8 23.5 all-gather.4
  251.8 37.5 reduce-scatter.1
where the time goes:
time: 298 us
  waiting for transfers between devices  233 us (78%)
  matrix products  39.3 us (13%)
  between operations  13.7 us (5%)
  local copies, waits for them, and re-layouts  6.61 us (2%)
  other arithmetic  5.32 us (2%)
    all_gather x1, waiting for transfers between devices, local(): grad_pre = lax.all_gather(local_grad, ('row', 'depth'), axis=0, tiled=True)  213 us
    dot_general x1, matrix products, local(): lax.dot_general(all_inputs, grad_pre, (((0,), (0,)), ((), ())), preferred...  19.9 us
    dot_general x1, matrix products, local(): lax.dot_general(grad_pre, weight_in, (((1,), (1,)), ((), ())), preferred_...  19.4 us
    reduce_scatter x1, waiting for transfers between devices, local(): lax.psum_scatter(partial_inputs, 'col', scatter_dimension=0, tiled=True)  13.4 us
    unnamed x1, local copies, waits for them, and re-layouts  6.61 us
  transfers between devices with their start and end apart: 3, of which 3 were waited for; matrix products, arithmetic and copies ran while one was open for 15% of the time, Pallas kernels for 0%

commit v1 on v0

v1 whole, which is shorter than its diff:
```python
import functools

import jax
import jax.numpy as jnp
from jax import lax
from jax.experimental import pallas as pl
from jax.experimental.pallas import tpu as pltpu
from jax.sharding import PartitionSpec as P

MESH = pl.DeviceIdType.MESH
WIDTH = 256
ROOT = 0.7978845608028654
CUBE = 0.044715


def gelu_back(grad_hidden, saved_pre):
    a = saved_pre.astype(jnp.float32)
    square = a * a
    t = jnp.tanh(ROOT * (a + CUBE * (square * a)))
    slope = 0.5 * (1.0 + t) + 0.5 * a * (1.0 - t * t) * (ROOT * (1.0 + (3.0 * CUBE) * square))
    return (grad_hidden.astype(jnp.float32) * slope).astype(jnp.bfloat16)


def kernel(ticks, x_ref, pre_ref, gh_ref, w_hbm, dx_ref, dw_hbm, gall, wv, xt, acc, dwv, from_core, to_side, from_side,
           g_send, g_recv, p_send, p_recv, x_send, x_recv, r_send, r_recv, w_sem, o_sem):
    y = lax.axis_index("row")
    col = lax.axis_index("col")
    depth = lax.axis_index("depth")
    side, core = col // 2, col % 2
    far, z = depth // 4, depth % 4
    y_up, y_down = (y + 1) % 4, (y + 3) % 4
    z_up, z_down = (z + 1) % 4, (z + 3) % 4
    y_dev = ((y_up, col, depth), (y_down, col, depth))
    z_dev = ((y, col, far * 4 + z_up), (y, col, far * 4 + z_down))
    far_dev = (y, col, (1 - far) * 4 + z)
    side_dev = (y, (1 - side) * 2 + core, depth)
    core_dev = (y, side * 2 + 1 - core, depth)
    rows, model = x_ref.shape
    pair = 2 * WIDTH

    load_w = pltpu.make_async_copy(w_hbm, wv, w_sem)
    load_w.start()

    barrier = pltpu.get_barrier_semaphore()
    for dev in (*y_dev, *z_dev, far_dev, side_dev, core_dev):
        pl.semaphore_signal(barrier, 1, device_id=dev, device_id_type=MESH)
    pl.semaphore_wait(barrier, 7)

    def remote(src, dst, send, recv, dev):
        return pltpu.make_async_remote_copy(src, dst, send, recv, device_id=dev, device_id_type=MESH)

    def far_copy(t, which):
        return remote(
            gall.at[t, :, y, far, z], gall.at[t, :, y, which, z], p_send.at[t], p_recv.at[t], far_dev
        )

    def places(t, stage, chunk, way):
        up = way == 0
        if chunk == 0:
            first_in, first_out = (y_down, y_up) if up else (y_up, y_down)
            second_in = z_down if up else z_up
            if stage == 0:
                return gall.at[t, 0, y, :, z], gall.at[t, 0, first_in, :, z], y_dev[way]
            if stage == 1:
                return gall.at[t, 0, first_in, way, z], gall.at[t, 0, (y + 2) % 4, way, z], y_dev[way]
            if stage == 2:
                return gall.at[t, 0, :, :, z], gall.at[t, 0, :, :, second_in], z_dev[way]
            return gall.at[t, 0, :, way, second_in], gall.at[t, 0, :, way, (z + 2) % 4], z_dev[way]
        first_in = z_down if up else z_up
        second_in = y_down if up else y_up
        if stage == 0:
            return gall.at[t, 1, y, :, z], gall.at[t, 1, y, :, first_in], z_dev[way]
        if stage == 1:
            return gall.at[t, 1, y, way, first_in], gall.at[t, 1, y, way, (z + 2) % 4], z_dev[way]
        if stage == 2:
            return gall.at[t, 1, y], gall.at[t, 1, second_in], y_dev[way]
        return gall.at[t, 1, second_in, way], gall.at[t, 1, (y + 2) % 4, way], y_dev[way]

    def start(t, stage):
        for chunk in range(2):
            for way in range(2):
                out, _, dev = places(t, stage, chunk, way)
                remote(out, out, g_send.at[t, stage, chunk, way], g_recv.at[t, stage, chunk, way], dev).start()

    def arrive(t, stage):
        for chunk in range(2):
            for way in range(2):
                _, come, dev = places(t, stage, chunk, way)
                remote(come, come, g_send.at[t, stage, chunk, way], g_recv.at[t, stage, chunk, way], dev).wait_recv()

    def sent(t, stage):
        for chunk in range(2):
            for way in range(2):
                out, _, dev = places(t, stage, chunk, way)
                remote(out, out, g_send.at[t, stage, chunk, way], g_recv.at[t, stage, chunk, way], dev).wait_send()

    def own_grad(t, carry):
        for chunk in range(2):
            cols = pl.ds(pl.multiple_of(t * pair + chunk * WIDTH, WIDTH), WIDTH)
            gall[t, chunk, y, far, z] = gelu_back(gh_ref[:, cols], pre_ref[:, cols])
        far_copy(t, far).start()
        return carry

    lax.fori_loop(0, ticks, own_grad, 0)

    own = pl.ds(pl.multiple_of(col * rows, rows), rows)
    beside = pl.ds(pl.multiple_of(((1 - side) * 2 + core) * rows, rows), rows)
    near = pl.ds(pl.multiple_of((side * 2 + 1 - core) * rows, rows), rows)
    cross = pl.ds(pl.multiple_of(((1 - side) * 2 + 1 - core) * rows, rows), rows)
    xt[:, own] = x_ref[...].T
    x_side = remote(xt.at[:, own], xt.at[:, own], x_send.at[0], x_recv.at[0], side_dev)
    x_core = remote(xt.at[:, own], xt.at[:, own], x_send.at[1], x_recv.at[1], core_dev)
    x_cross = remote(xt.at[:, beside], xt.at[:, beside], x_send.at[2], x_recv.at[2], core_dev)
    x_side.start()
    x_core.start()

    acc[...] = jnp.zeros_like(acc)

    def dx_part(t, owner):
        total = acc[owner]
        for chunk in range(2):
            cols = pl.ds(pl.multiple_of(t * pair + chunk * WIDTH, WIDTH), WIDTH)
            g = gall[t, chunk, owner].reshape(rows, WIDTH)
            total += lax.dot_general(g, wv[:, cols], (((1,), (1,)), ((), ())), preferred_element_type=jnp.float32)
        acc[owner] = total

    def dw_store(t):
        cols = pl.ds(pl.multiple_of(t * pair, pair), pair)
        return pltpu.make_async_copy(dwv.at[t], dw_hbm.at[:, cols], o_sem.at[t])

    def dw_part(t):
        for chunk in range(2):
            g = gall[t, chunk].reshape(4 * rows, WIDTH)
            dwv[t, :, pl.ds(chunk * WIDTH, WIDTH)] = jnp.dot(
                xt[...], g, preferred_element_type=jnp.float32
            ).astype(jnp.bfloat16)
        dw_store(t).start()

    def advance(t):
        @pl.when(t + 3 < ticks)
        def _():
            far_copy(t + 3, 1 - far).wait_recv()
            start(t + 3, 0)

        @pl.when(t >= 0)
        def _():
            arrive(t, 2)
            start(t, 3)

        @pl.when(jnp.logical_and(t + 1 >= 0, t + 1 < ticks))
        def _():
            arrive(t + 1, 1)
            start(t + 1, 2)

        @pl.when(jnp.logical_and(t + 2 >= 0, t + 2 < ticks))
        def _():
            arrive(t + 2, 0)
            start(t + 2, 1)

    def fill(i, carry):
        advance(i - 3)
        return carry

    lax.fori_loop(0, 3, fill, 0)

    beside_in = remote(xt.at[:, beside], xt.at[:, beside], x_send.at[0], x_recv.at[0], side_dev)
    near_in = remote(xt.at[:, near], xt.at[:, near], x_send.at[1], x_recv.at[1], core_dev)
    cross_in = remote(xt.at[:, cross], xt.at[:, cross], x_send.at[2], x_recv.at[2], core_dev)
    beside_in.wait_recv()
    x_cross.start()
    near_in.wait_recv()
    cross_in.wait_recv()
    load_w.wait()

    def tick(t, carry):
        advance(t)
        arrive(t, 3)

        def one(owner, c):
            dx_part(t, owner)
            return c

        lax.fori_loop(0, 4, one, 0)
        dw_part(t)
        return carry

    lax.fori_loop(0, ticks - 1, tick, 0)

    last = ticks - 1
    advance(last)
    arrive(last, 3)

    def owner_of(s, c):
        return s * 2 + c

    give = []
    for k, s in enumerate((1 - side, side)):
        j = owner_of(s, 1 - core)
        dx_part(last, j)
        copy = remote(acc.at[j], from_core.at[k], r_send.at[k], r_recv.at[k], core_dev)
        copy.start()
        give.append(copy)
    dx_part(last, owner_of(1 - side, core))
    give[0].wait_recv()
    to_side[...] = (acc[owner_of(1 - side, core)] + from_core[0]).astype(jnp.bfloat16)
    across = remote(to_side, from_side, r_send.at[2], r_recv.at[2], side_dev)
    across.start()
    dx_part(last, owner_of(side, core))
    dw_part(last)
    give[1].wait_recv()
    across.wait_recv()
    dx_ref[...] = (acc[owner_of(side, core)] + from_core[1] + from_side[...].astype(jnp.float32)).astype(jnp.bfloat16)

    def finish(t, carry):
        far_copy(t, far).wait_send()
        for stage in range(4):
            sent(t, stage)
        dw_store(t).wait()
        return carry

    lax.fori_loop(0, ticks, finish, 0)
    x_side.wait_send()
    x_core.wait_send()
    x_cross.wait_send()
    for copy in give:
        copy.wait_send()
    across.wait_send()


def local(inputs, weight_in, saved_pre, grad_hidden):
    rows, model = inputs.shape
    tokens, hidden = saved_pre.shape
    ticks = hidden // (2 * WIDTH)
    vmem = pl.BlockSpec(memory_space=pltpu.VMEM)
    hbm = pl.BlockSpec(memory_space=pl.ANY)
    dma = pltpu.SemaphoreType.DMA
    return pl.pallas_call(
        functools.partial(kernel, ticks),
        out_shape=(
            jax.ShapeDtypeStruct((rows, model), jnp.bfloat16),
            jax.ShapeDtypeStruct((model, hidden), jnp.bfloat16),
        ),
        in_specs=[vmem, vmem, vmem, hbm],
        out_specs=(vmem, hbm),
        scratch_shapes=[
            pltpu.VMEM((ticks, 2, 4, 2, 4, tokens, WIDTH), jnp.bfloat16),
            pltpu.VMEM((model, hidden), jnp.bfloat16),
            pltpu.VMEM((model, 4 * rows), jnp.bfloat16),
            pltpu.VMEM((4, rows, model), jnp.float32),
            pltpu.VMEM((ticks, model, 2 * WIDTH), jnp.bfloat16),
            pltpu.VMEM((2, rows, model), jnp.float32),
            pltpu.VMEM((rows, model), jnp.bfloat16),
            pltpu.VMEM((rows, model), jnp.bfloat16),
            dma((ticks, 4, 2, 2)),
            dma((ticks, 4, 2, 2)),
            dma((ticks,)),
            dma((ticks,)),
            dma((3,)),
            dma((3,)),
            dma((3,)),
            dma((3,)),
            dma,
            dma((ticks,)),
        ],
        compiler_params=pltpu.CompilerParams(
            collective_id=0, has_side_effects=True, vmem_limit_bytes=60 * 2**20
        ),
        name="gather_and_multiply",
    )(inputs, saved_pre, grad_hidden, weight_in)


def solution(mesh):
    return jax.shard_map(
        local,
        mesh=mesh,
        in_specs=(
            P("col", ("row", "depth")),
            P(("row", "depth"), "col"),
            P(("row", "depth"), "col"),
            P(("row", "depth"), "col"),
        ),
        out_specs=(P("col", ("row", "depth")), P(("row", "depth"), "col")),
        check_vma=False,
    )
```

time: 298 us -> 186 us (0.62)
  waiting for transfers between devices: 233 us -> 0 us
  Pallas kernels: 0 us -> 178 us
  matrix products: 39.3 us -> 0 us
  between operations: 13.7 us -> 0.64 us
  other arithmetic: 5.32 us -> 0 us
    all_gather x2 -> x0, waiting for transfers between devices: 219 us -> none  [the longest x1 213 us: local(): grad_pre = lax.all_gather(local_grad, ('row', 'depth'), axis=0, tiled=True)]
    pallas_call x0 -> x1, Pallas kernels: none -> 178 us  [local(): pl.pallas_call(functools.partial(kernel, ticks), out_shape=(jax.ShapeDtyp...]
    dot_general x2 -> x0, matrix products: 39.3 us -> none  [the longest x1 19.9 us: local(): lax.dot_general(all_inputs, grad_pre, (((0,), (0,)), ((), ())), preferred...]
    reduce_scatter x1 -> x0, waiting for transfers between devices: 13.4 us -> none  [local(): lax.psum_scatter(partial_inputs, 'col', scatter_dimension=0, tiled=True)]
    convert_element_type x2 -> x0, other arithmetic: 5.32 us -> none  [the longest x1 3.39 us: gelu_back(): return pull(grad_hidden.astype(jnp.float32))[0].astype(jnp.bfloat16)]
    unnamed x1 -> x2, local copies, waits for them, and re-layouts: 6.61 us -> 6.83 us
  transfers between devices with their start and end apart: 3 -> 0, of which waited for: 3 -> 0; matrix products, arithmetic and copies ran while one was open for 15% -> 0% of each run, Pallas kernels for 0% -> 0%
where the time goes in v1:
time: 186 us
  Pallas kernels  178 us (96%)
  local copies, waits for them, and re-layouts  6.83 us (4%)
    pallas_call x1, Pallas kernels, local(): pl.pallas_call(functools.partial(kernel, ticks), out_shape=(jax.ShapeDtyp...  178 us
    unnamed x2, local copies, waits for them, and re-layouts  6.83 us

profile of v1, /device:TPU:1, one launch (start us, length us, event | category | flops | bytes accessed | tf_op | source)
XLA Modules:
  0.0 185.5 jit_solution(15023949383629442893)
XLA Ops:
  0.6 178.0 %gather_and_multiply.1 = (bf16[512,384]{1,0:T(8,128)(2,1)}, bf16[384,6144]{1,0:T(8,128)(2,1)}) custom-call(bf16[512,384]{1,0:T(8,128)(2,1)} %x_ref.1, bf16[64,6144]{1,0:T(8,128)(2,1)} %pre_ref.1, bf16[64,6144]{1,0:T(8,128)(2,1)} %gh_ref.1, bf16[384,6144]{1,0:T(8,128)(2,1)} %w_hbm.1), custom_call_target="tpu_custom_call" | custom-call | tf_op jit(solution)/shard_map/gather_and_multiply/pallas_call | solution.py:237
  178.7 1.8 copy.8
  180.5 5.1 %copy.9 = bf16[384,6144]{1,0:T(8,128)(2,1)} copy(bf16[384,6144]{1,0:T(8,128)(2,1)} %get-tuple-element.5) | data formatting | bytes 9437184

commit v2 on v1

v2 whole, which is shorter than its diff:
```python
import functools

import jax
import jax.numpy as jnp
from jax import lax
from jax.experimental import pallas as pl
from jax.experimental.pallas import tpu as pltpu
from jax.sharding import PartitionSpec as P

MESH = pl.DeviceIdType.MESH
WIDTH = 256
LEAD = (3, 2, 1, 0)
LAG = 1
PAIRED = 3
BEFORE = 2
ROOT = 0.7978845608028654
CUBE = 0.044715


def gelu_back(grad_hidden, saved_pre):
    a = saved_pre.astype(jnp.float32)
    square = a * a
    t = jnp.tanh(ROOT * (a + CUBE * (square * a)))
    slope = 0.5 * (1.0 + t) + 0.5 * a * (1.0 - t * t) * (ROOT * (1.0 + (3.0 * CUBE) * square))
    return (grad_hidden.astype(jnp.float32) * slope).astype(jnp.bfloat16)


def kernel(ticks, x_ref, pre_ref, gh_ref, w_hbm, dx_ref, dw_hbm, gall, gout, wv, wp, xt, xtp, acc, accp, dwv, dwp,
           from_core, from_core_p, to_chips, from_chips, g_send, g_recv, p_send, p_recv, x_send, x_recv, r_send, r_recv,
           wp_send, wp_recv, dwp_send, dwp_recv, w_sem, o_sem):
    y = lax.axis_index("row")
    col = lax.axis_index("col")
    depth = lax.axis_index("depth")
    side, core = col // 2, col % 2
    far, z = depth // 4, depth % 4
    y_up, y_down = (y + 1) % 4, (y + 3) % 4
    z_up, z_down = (z + 1) % 4, (z + 3) % 4
    y_dev = ((y_up, col, depth), (y_down, col, depth))
    z_dev = ((y, col, far * 4 + z_up), (y, col, far * 4 + z_down))
    far_dev = (y, col, (1 - far) * 4 + z)
    side_dev = (y, (1 - side) * 2 + core, depth)
    core_dev = (y, side * 2 + 1 - core, depth)
    diag_dev = (y, (1 - side) * 2 + core, (1 - far) * 4 + z)
    rows, model = x_ref.shape
    pair = 2 * WIDTH

    load_w = pltpu.make_async_copy(w_hbm, wv, w_sem)
    load_w.start()

    barrier = pltpu.get_barrier_semaphore()
    for dev in (*y_dev, *z_dev, far_dev, side_dev, core_dev, diag_dev):
        pl.semaphore_signal(barrier, 1, device_id=dev, device_id_type=MESH)
    pl.semaphore_wait(barrier, 8)

    def remote(src, dst, send, recv, dev):
        return pltpu.make_async_remote_copy(src, dst, send, recv, device_id=dev, device_id_type=MESH)

    def far_in(t):
        place = gall.at[t, :, y, 1 - far, z]
        return remote(place, place, p_send.at[t], p_recv.at[t], far_dev)

    def early(t):
        return pl.multiple_of(t * pair, pair)

    def mine(t):
        return pl.multiple_of((t + far * PAIRED) * pair, pair)

    def theirs(t):
        return pl.multiple_of((t + (1 - far) * PAIRED) * pair, pair)

    def late(t):
        return pl.multiple_of((t + PAIRED) * pair, pair)

    def places(t, stage, chunk, way):
        up = way == 0
        if chunk == 0:
            first_in, first_out = (y_down, y_up) if up else (y_up, y_down)
            second_in = z_down if up else z_up
            if stage == 0:
                return gall.at[t, 0, y, :, z], gall.at[t, 0, first_in, :, z], y_dev[way]
            if stage == 1:
                return gall.at[t, 0, first_in, way, z], gall.at[t, 0, (y + 2) % 4, way, z], y_dev[way]
            if stage == 2:
                return gall.at[t, 0, :, :, z], gall.at[t, 0, :, :, second_in], z_dev[way]
            return gall.at[t, 0, :, way, second_in], gall.at[t, 0, :, way, (z + 2) % 4], z_dev[way]
        first_in = z_down if up else z_up
        second_in = y_down if up else y_up
        if stage == 0:
            return gall.at[t, 1, y, :, z], gall.at[t, 1, y, :, first_in], z_dev[way]
        if stage == 1:
            return gall.at[t, 1, y, way, first_in], gall.at[t, 1, y, way, (z + 2) % 4], z_dev[way]
        if stage == 2:
            return gall.at[t, 1, y], gall.at[t, 1, second_in], y_dev[way]
        return gall.at[t, 1, second_in, way], gall.at[t, 1, (y + 2) % 4, way], y_dev[way]

    def start(t, stage):
        for chunk in range(2):
            for way in range(2):
                out, _, dev = places(t, stage, chunk, way)
                remote(out, out, g_send.at[t, stage, chunk, way], g_recv.at[t, stage, chunk, way], dev).start()

    def arrive(t, stage):
        for chunk in range(2):
            for way in range(2):
                _, come, dev = places(t, stage, chunk, way)
                remote(come, come, g_send.at[t, stage, chunk, way], g_recv.at[t, stage, chunk, way], dev).wait_recv()

    def sent(t, stage):
        for chunk in range(2):
            for way in range(2):
                out, _, dev = places(t, stage, chunk, way)
                remote(out, out, g_send.at[t, stage, chunk, way], g_recv.at[t, stage, chunk, way], dev).wait_send()

    def grad_at(base, chunk):
        cols = pl.ds(pl.multiple_of(base + chunk * WIDTH, WIDTH), WIDTH)
        return gelu_back(gh_ref[:, cols], pre_ref[:, cols])

    def own_grad(place, t, carry):
        for chunk in range(2):
            gall[t, chunk, y, far, z] = grad_at(place(t), chunk)
        out = gall.at[t, :, y, far, z]
        remote(out, out, p_send.at[t], p_recv.at[t], far_dev).start()
        return carry

    def paired_grad(t, carry):
        for chunk in range(2):
            gout[t - BEFORE, chunk] = grad_at(theirs(t), chunk)
        remote(gout.at[t - BEFORE], gall.at[t, :, y, far, z], p_send.at[t], p_recv.at[t], far_dev).start()
        for chunk in range(2):
            gall[t, chunk, y, far, z] = grad_at(mine(t), chunk)
        return carry

    after = BEFORE + PAIRED
    lax.fori_loop(0, BEFORE, functools.partial(own_grad, early), 0)
    lax.fori_loop(BEFORE, after, paired_grad, 0)
    lax.fori_loop(after, ticks, functools.partial(own_grad, late), 0)

    own = pl.ds(pl.multiple_of(col * rows, rows), rows)
    beside = pl.ds(pl.multiple_of(((1 - side) * 2 + core) * rows, rows), rows)
    near = pl.ds(pl.multiple_of((side * 2 + 1 - core) * rows, rows), rows)
    cross = pl.ds(pl.multiple_of(((1 - side) * 2 + 1 - core) * rows, rows), rows)
    xt[:, own] = x_ref[...].T

    def x_copy(k, src, dst, dev):
        return remote(src, dst, x_send.at[k], x_recv.at[k], dev)

    x_out = [
        x_copy(0, xt.at[:, own], xt.at[:, own], side_dev),
        x_copy(1, xt.at[:, own], xt.at[:, own], core_dev),
        x_copy(2, xt.at[:, own], xtp.at[:, own], far_dev),
        x_copy(3, xt.at[:, own], xtp.at[:, own], diag_dev),
        x_copy(4, xt.at[:, beside], xt.at[:, beside], core_dev),
        x_copy(5, xtp.at[:, own], xtp.at[:, own], core_dev),
        x_copy(6, xtp.at[:, beside], xtp.at[:, beside], core_dev),
    ]
    x_in = [
        x_copy(0, xt.at[:, beside], xt.at[:, beside], side_dev),
        x_copy(1, xt.at[:, near], xt.at[:, near], core_dev),
        x_copy(2, xtp.at[:, own], xtp.at[:, own], far_dev),
        x_copy(3, xtp.at[:, beside], xtp.at[:, beside], diag_dev),
        x_copy(4, xt.at[:, cross], xt.at[:, cross], core_dev),
        x_copy(5, xtp.at[:, near], xtp.at[:, near], core_dev),
        x_copy(6, xtp.at[:, cross], xtp.at[:, cross], core_dev),
    ]
    for copy in x_out[:4]:
        copy.start()

    def wp_copy(k):
        return remote(
            w_hbm.at[:, pl.ds(theirs(k + BEFORE), pair)], wp.at[k], wp_send.at[k], wp_recv.at[k], far_dev
        )

    def send_weights(k, carry):
        wp_copy(k).start()
        return carry

    lax.fori_loop(0, PAIRED, send_weights, 0)

    accp[...] = jnp.zeros_like(accp)
    acc[...] = jnp.zeros_like(acc)

    def dx_part(t, base, owner):
        total = acc[owner]
        for chunk in range(2):
            cols = pl.ds(pl.multiple_of(base + chunk * WIDTH, WIDTH), WIDTH)
            g = gall[t, chunk, owner].reshape(rows, WIDTH)
            total += lax.dot_general(g, wv[:, cols], (((1,), (1,)), ((), ())), preferred_element_type=jnp.float32)
        acc[owner] = total

    def dxp_part(t, owner):
        total = accp[owner]
        for chunk in range(2):
            w = wp[t - BEFORE, :, pl.ds(chunk * WIDTH, WIDTH)]
            g = gall[t, chunk, owner].reshape(rows, WIDTH)
            total += lax.dot_general(g, w, (((1,), (1,)), ((), ())), preferred_element_type=jnp.float32)
        accp[owner] = total

    def dw_store(t, base):
        return pltpu.make_async_copy(dwv.at[t], dw_hbm.at[:, pl.ds(base, pair)], o_sem.at[t])

    def dw_part(t, base):
        for chunk in range(2):
            g = gall[t, chunk].reshape(4 * rows, WIDTH)
            dwv[t, :, pl.ds(chunk * WIDTH, WIDTH)] = jnp.dot(
                xt[...], g, preferred_element_type=jnp.float32
            ).astype(jnp.bfloat16)
        dw_store(t, base).start()

    def dwp_copy(t, base):
        k = t - BEFORE
        return remote(dwp.at[k], dw_hbm.at[:, pl.ds(base, pair)], dwp_send.at[k], dwp_recv.at[k], far_dev)

    def dwp_part(t):
        for chunk in range(2):
            g = gall[t, chunk].reshape(4 * rows, WIDTH)
            dwp[t - BEFORE, :, pl.ds(chunk * WIDTH, WIDTH)] = jnp.dot(
                xtp[...], g, preferred_element_type=jnp.float32
            ).astype(jnp.bfloat16)
        dwp_copy(t, mine(t)).start()

    def advance(i):
        @pl.when(i + LEAD[0] < ticks)
        def _():
            far_in(i + LEAD[0]).wait_recv()
            start(i + LEAD[0], 0)

        for stage in range(1, 4):
            t = i + LEAD[stage]

            @pl.when(jnp.logical_and(t >= 0, t < ticks))
            def _(t=t, stage=stage):
                arrive(t, stage - 1)
                start(t, stage)

    def fill(i, carry):
        advance(i - LEAD[0])
        return carry

    lax.fori_loop(0, LEAD[0] + LAG, fill, 0)

    x_in[0].wait_recv()
    x_out[4].start()
    x_in[1].wait_recv()
    x_in[4].wait_recv()
    load_w.wait()

    def tick(place, t, carry):
        advance(t + LAG)
        arrive(t, 3)

        def one(owner, c):
            dx_part(t, place(t), owner)
            return c

        lax.fori_loop(0, 4, one, 0)
        dw_part(t, place(t))
        return carry

    def paired_tick(t, carry):
        advance(t + LAG)
        arrive(t, 3)
        wp_copy(t - BEFORE).wait_recv()
        dwp_part(t)

        def one(owner, c):
            dxp_part(t, owner)
            dx_part(t, mine(t), owner)
            return c

        lax.fori_loop(0, 4, one, 0)
        dw_part(t, mine(t))
        return carry

    lax.fori_loop(0, BEFORE, functools.partial(tick, early), 0)

    for k in (2, 3):
        x_in[k].wait_recv()
        x_out[k + 3].start()
    x_in[5].wait_recv()
    x_in[6].wait_recv()

    lax.fori_loop(BEFORE, after, paired_tick, 0)

    give = []
    for k, s in enumerate((1 - side, side)):
        copy = remote(accp.at[s * 2 + 1 - core], from_core_p.at[k], r_send.at[k], r_recv.at[k], core_dev)
        copy.start()
        give.append(copy)
    for k, (s, dev) in enumerate(((1 - side, diag_dev), (side, far_dev))):
        give[k].wait_recv()
        to_chips[k] = (accp[s * 2 + core] + from_core_p[k]).astype(jnp.bfloat16)
        copy = remote(to_chips.at[k], from_chips.at[k], r_send.at[2 + k], r_recv.at[2 + k], dev)
        copy.start()
        give.append(copy)

    last = ticks - 1
    lax.fori_loop(after, last, functools.partial(tick, late), 0)

    advance(last + LAG)
    arrive(last, 3)

    def owner_of(s, c):
        return s * 2 + c

    for k, s in enumerate((1 - side, side)):
        j = owner_of(s, 1 - core)
        dx_part(last, late(last), j)
        copy = remote(acc.at[j], from_core.at[k], r_send.at[4 + k], r_recv.at[4 + k], core_dev)
        copy.start()
        give.append(copy)
    dx_part(last, late(last), owner_of(1 - side, core))
    give[4].wait_recv()
    to_chips[2] = (acc[owner_of(1 - side, core)] + from_core[0]).astype(jnp.bfloat16)
    across = remote(to_chips.at[2], from_chips.at[2], r_send.at[6], r_recv.at[6], side_dev)
    across.start()
    give.append(across)
    dx_part(last, late(last), owner_of(side, core))
    dw_part(last, late(last))
    give[5].wait_recv()
    give[2].wait_recv()
    give[3].wait_recv()
    total = acc[owner_of(side, core)] + from_core[1]
    total += from_chips[0].astype(jnp.float32) + from_chips[1].astype(jnp.float32)
    across.wait_recv()
    dx_ref[...] = (total + from_chips[2].astype(jnp.float32)).astype(jnp.bfloat16)

    def finish(t, carry):
        far_in(t).wait_send()
        for stage in range(4):
            sent(t, stage)
        return carry

    def stored(place, t, carry):
        dw_store(t, place(t)).wait()
        return carry

    def exchanged(t, carry):
        wp_copy(t - BEFORE).wait_send()
        dwp_copy(t, theirs(t)).wait()
        return carry

    lax.fori_loop(0, ticks, finish, 0)
    lax.fori_loop(0, BEFORE, functools.partial(stored, early), 0)
    lax.fori_loop(BEFORE, after, functools.partial(stored, mine), 0)
    lax.fori_loop(after, ticks, functools.partial(stored, late), 0)
    lax.fori_loop(BEFORE, after, exchanged, 0)
    for copy in x_out:
        copy.wait_send()
    for copy in give:
        copy.wait_send()


def local(inputs, weight_in, saved_pre, grad_hidden):
    rows, model = inputs.shape
    tokens, hidden = saved_pre.shape
    pair = 2 * WIDTH
    ticks = hidden // pair - PAIRED
    vmem = pl.BlockSpec(memory_space=pltpu.VMEM)
    hbm = pl.BlockSpec(memory_space=pl.ANY)
    dma = pltpu.SemaphoreType.DMA
    return pl.pallas_call(
        functools.partial(kernel, ticks),
        out_shape=(
            jax.ShapeDtypeStruct((rows, model), jnp.bfloat16),
            jax.ShapeDtypeStruct((model, hidden), jnp.bfloat16),
        ),
        in_specs=[vmem, vmem, vmem, hbm],
        out_specs=(vmem, hbm),
        scratch_shapes=[
            pltpu.VMEM((ticks, 2, 4, 2, 4, tokens, WIDTH), jnp.bfloat16),
            pltpu.VMEM((PAIRED, 2, tokens, WIDTH), jnp.bfloat16),
            pltpu.VMEM((model, hidden), jnp.bfloat16),
            pltpu.VMEM((PAIRED, model, pair), jnp.bfloat16),
            pltpu.VMEM((model, 4 * rows), jnp.bfloat16),
            pltpu.VMEM((model, 4 * rows), jnp.bfloat16),
            pltpu.VMEM((4, rows, model), jnp.float32),
            pltpu.VMEM((4, rows, model), jnp.float32),
            pltpu.VMEM((ticks, model, pair), jnp.bfloat16),
            pltpu.VMEM((PAIRED, model, pair), jnp.bfloat16),
            pltpu.VMEM((2, rows, model), jnp.float32),
            pltpu.VMEM((2, rows, model), jnp.float32),
            pltpu.VMEM((3, rows, model), jnp.bfloat16),
            pltpu.VMEM((3, rows, model), jnp.bfloat16),
            dma((ticks, 4, 2, 2)),
            dma((ticks, 4, 2, 2)),
            dma((ticks,)),
            dma((ticks,)),
            dma((7,)),
            dma((7,)),
            dma((7,)),
            dma((7,)),
            dma((PAIRED,)),
            dma((PAIRED,)),
            dma((PAIRED,)),
            dma((PAIRED,)),
            dma,
            dma((ticks,)),
        ],
        compiler_params=pltpu.CompilerParams(
            collective_id=0, has_side_effects=True, vmem_limit_bytes=60 * 2**20
        ),
        name="gather_and_multiply",
    )(inputs, saved_pre, grad_hidden, weight_in)


def solution(mesh):
    return jax.shard_map(
        local,
        mesh=mesh,
        in_specs=(
            P("col", ("row", "depth")),
            P(("row", "depth"), "col"),
            P(("row", "depth"), "col"),
            P(("row", "depth"), "col"),
        ),
        out_specs=(P("col", ("row", "depth")), P(("row", "depth"), "col")),
        check_vma=False,
    )
```

time: 186 us -> 136 us (0.73)
  Pallas kernels: 178 us -> 129 us
    pallas_call x1, Pallas kernels: 178 us -> 129 us  [local(): pl.pallas_call(functools.partial(kernel, ticks), out_shape=(jax.ShapeDtyp...]
where the time goes in v2:
time: 136 us
  Pallas kernels  129 us (95%)
  local copies, waits for them, and re-layouts  6.83 us (5%)
    pallas_call x1, Pallas kernels, local(): pl.pallas_call(functools.partial(kernel, ticks), out_shape=(jax.ShapeDtyp...  129 us
    unnamed x2, local copies, waits for them, and re-layouts  6.83 us

profile of v2, /device:TPU:1, one launch (start us, length us, event | category | flops | bytes accessed | tf_op | source)
XLA Modules:
  0.0 136.1 jit_solution(9132750383672135315)
XLA Ops:
  0.6 128.7 %gather_and_multiply.1 = (bf16[512,384]{1,0:T(8,128)(2,1)}, bf16[384,6144]{1,0:T(8,128)(2,1)}) custom-call(bf16[512,384]{1,0:T(8,128)(2,1)} %x_ref.1, bf16[64,6144]{1,0:T(8,128)(2,1)} %pre_ref.1, bf16[64,6144]{1,0:T(8,128)(2,1)} %gh_ref.1, bf16[384,6144]{1,0:T(8,128)(2,1)} %w_hbm.1), custom_call_target="tpu_custom_call" | custom-call | tf_op jit(solution)/shard_map/gather_and_multiply/pallas_call | solution.py:361
  129.3 1.8 %copy.8 = bf16[512,384]{1,0:T(8,128)(2,1)} copy(bf16[512,384]{1,0:T(8,128)(2,1)} %get-tuple-element.4) | data formatting | bytes 786432
  131.1 5.1 %copy.9 = bf16[384,6144]{1,0:T(8,128)(2,1)} copy(bf16[384,6144]{1,0:T(8,128)(2,1)} %get-tuple-element.5) | data formatting | bytes 9437184

commit v3 on v2

--- a/solution.py
+++ b/solution.py
@@ -12,7 +12,7 @@
 LEAD = (3, 2, 1, 0)
 LAG = 1
 PAIRED = 3
-BEFORE = 2
+BEFORE = 1
 ROOT = 0.7978845608028654
 CUBE = 0.044715
 
@@ -25,9 +25,9 @@
     return (grad_hidden.astype(jnp.float32) * slope).astype(jnp.bfloat16)
 
 
-def kernel(ticks, x_ref, pre_ref, gh_ref, w_hbm, dx_ref, dw_hbm, gall, gout, wv, wp, xt, xtp, acc, accp, dwv, dwp,
+def kernel(ticks, x_ref, pre_ref, gh_ref, w_hbm, dx_ref, dw_ref, gall, gout, wv, wp, xt, xtp, acc, accp, dwp,
            from_core, from_core_p, to_chips, from_chips, g_send, g_recv, p_send, p_recv, x_send, x_recv, r_send, r_recv,
-           wp_send, wp_recv, dwp_send, dwp_recv, w_sem, o_sem):
+           wp_send, wp_recv, dwp_send, dwp_recv, w_sem):
     y = lax.axis_index("row")
     col = lax.axis_index("col")
     depth = lax.axis_index("depth")
@@ -50,7 +50,6 @@
     barrier = pltpu.get_barrier_semaphore()
     for dev in (*y_dev, *z_dev, far_dev, side_dev, core_dev, diag_dev):
         pl.semaphore_signal(barrier, 1, device_id=dev, device_id_type=MESH)
-    pl.semaphore_wait(barrier, 8)
 
     def remote(src, dst, send, recv, dev):
         return pltpu.make_async_remote_copy(src, dst, send, recv, device_id=dev, device_id_type=MESH)
@@ -76,8 +75,9 @@
         if chunk == 0:
             first_in, first_out = (y_down, y_up) if up else (y_up, y_down)
             second_in = z_down if up else z_up
-            if stage == 0:
-                return gall.at[t, 0, y, :, z], gall.at[t, 0, first_in, :, z], y_dev[way]
+            if stage in (0, 4):
+                half = far if stage == 4 else 1 - far
+                return gall.at[t, 0, y, half, z], gall.at[t, 0, first_in, half, z], y_dev[way]
             if stage == 1:
                 return gall.at[t, 0, first_in, way, z], gall.at[t, 0, (y + 2) % 4, way, z], y_dev[way]
             if stage == 2:
@@ -85,8 +85,9 @@
             return gall.at[t, 0, :, way, second_in], gall.at[t, 0, :, way, (z + 2) % 4], z_dev[way]
         first_in = z_down if up else z_up
         second_in = y_down if up else y_up
-        if stage == 0:
-            return gall.at[t, 1, y, :, z], gall.at[t, 1, y, :, first_in], z_dev[way]
+        if stage in (0, 4):
+            half = far if stage == 4 else 1 - far
+            return gall.at[t, 1, y, half, z], gall.at[t, 1, y, half, first_in], z_dev[way]
         if stage == 1:
             return gall.at[t, 1, y, way, first_in], gall.at[t, 1, y, way, (z + 2) % 4], z_dev[way]
         if stage == 2:
@@ -118,15 +119,11 @@
     def own_grad(place, t, carry):
         for chunk in range(2):
             gall[t, chunk, y, far, z] = grad_at(place(t), chunk)
-        out = gall.at[t, :, y, far, z]
-        remote(out, out, p_send.at[t], p_recv.at[t], far_dev).start()
         return carry
 
     def paired_grad(t, carry):
         for chunk in range(2):
             gout[t - BEFORE, chunk] = grad_at(theirs(t), chunk)
-        remote(gout.at[t - BEFORE], gall.at[t, :, y, far, z], p_send.at[t], p_recv.at[t], far_dev).start()
-        for chunk in range(2):
             gall[t, chunk, y, far, z] = grad_at(mine(t), chunk)
         return carry
 
@@ -134,36 +131,56 @@
     lax.fori_loop(0, BEFORE, functools.partial(own_grad, early), 0)
     lax.fori_loop(BEFORE, after, paired_grad, 0)
     lax.fori_loop(after, ticks, functools.partial(own_grad, late), 0)
+    own = pl.ds(pl.multiple_of(col * rows, rows), rows)
+    xt[:, own] = x_ref[...].T
+    pl.semaphore_wait(barrier, 8)
+
+    def own_out(t, carry):
+        out = gall.at[t, :, y, far, z]
+        remote(out, out, p_send.at[t], p_recv.at[t], far_dev).start()
+        start(t, 4)
+        return carry
+
+    def paired_out(t, carry):
+        remote(gout.at[t - BEFORE], gall.at[t, :, y, far, z], p_send.at[t], p_recv.at[t], far_dev).start()
+        start(t, 4)
+        return carry
+
+    lax.fori_loop(0, BEFORE, own_out, 0)
+    lax.fori_loop(BEFORE, after, paired_out, 0)
 
     own = pl.ds(pl.multiple_of(col * rows, rows), rows)
     beside = pl.ds(pl.multiple_of(((1 - side) * 2 + core) * rows, rows), rows)
     near = pl.ds(pl.multiple_of((side * 2 + 1 - core) * rows, rows), rows)
     cross = pl.ds(pl.multiple_of(((1 - side) * 2 + 1 - core) * rows, rows), rows)
-    xt[:, own] = x_ref[...].T
 
     def x_copy(k, src, dst, dev):
         return remote(src, dst, x_send.at[k], x_recv.at[k], dev)
 
+    low, high = pl.ds(0, model // 2), pl.ds(model // 2, model // 2)
     x_out = [
         x_copy(0, xt.at[:, own], xt.at[:, own], side_dev),
-        x_copy(1, xt.at[:, own], xt.at[:, own], core_dev),
-        x_copy(2, xt.at[:, own], xtp.at[:, own], far_dev),
-        x_copy(3, xt.at[:, own], xtp.at[:, own], diag_dev),
-        x_copy(4, xt.at[:, beside], xt.at[:, beside], core_dev),
-        x_copy(5, xtp.at[:, own], xtp.at[:, own], core_dev),
+        x_copy(1, xt.at[:, own], xtp.at[:, own], diag_dev),
+        x_copy(2, xt.at[:, own], xt.at[:, own], core_dev),
+        x_copy(3, xt.at[low, own], xtp.at[low, own], far_dev),
+        x_copy(4, xt.at[high, own], xtp.at[high, own], far_dev),
+        x_copy(5, xt.at[:, beside], xt.at[:, beside], core_dev),
         x_copy(6, xtp.at[:, beside], xtp.at[:, beside], core_dev),
+        x_copy(7, xtp.at[:, own], xtp.at[:, own], core_dev),
     ]
     x_in = [
         x_copy(0, xt.at[:, beside], xt.at[:, beside], side_dev),
-        x_copy(1, xt.at[:, near], xt.at[:, near], core_dev),
-        x_copy(2, xtp.at[:, own], xtp.at[:, own], far_dev),
-        x_copy(3, xtp.at[:, beside], xtp.at[:, beside], diag_dev),
-        x_copy(4, xt.at[:, cross], xt.at[:, cross], core_dev),
-        x_copy(5, xtp.at[:, near], xtp.at[:, near], core_dev),
+        x_copy(1, xtp.at[:, beside], xtp.at[:, beside], diag_dev),
+        x_copy(2, xt.at[:, near], xt.at[:, near], core_dev),
+        x_copy(3, xtp.at[low, own], xtp.at[low, own], diag_dev),
+        x_copy(4, xtp.at[high, own], xtp.at[high, own], side_dev),
+        x_copy(5, xt.at[:, cross], xt.at[:, cross], core_dev),
         x_copy(6, xtp.at[:, cross], xtp.at[:, cross], core_dev),
+        x_copy(7, xtp.at[:, near], xtp.at[:, near], core_dev),
     ]
-    for copy in x_out[:4]:
+    for copy in x_out[:5]:
         copy.start()
+    lax.fori_loop(after, ticks, own_out, 0)
 
     def wp_copy(k):
         return remote(
@@ -195,20 +212,17 @@
             total += lax.dot_general(g, w, (((1,), (1,)), ((), ())), preferred_element_type=jnp.float32)
         accp[owner] = total
 
-    def dw_store(t, base):
-        return pltpu.make_async_copy(dwv.at[t], dw_hbm.at[:, pl.ds(base, pair)], o_sem.at[t])
-
     def dw_part(t, base):
         for chunk in range(2):
             g = gall[t, chunk].reshape(4 * rows, WIDTH)
-            dwv[t, :, pl.ds(chunk * WIDTH, WIDTH)] = jnp.dot(
+            cols = pl.ds(pl.multiple_of(base + chunk * WIDTH, WIDTH), WIDTH)
+            dw_ref[:, cols] = jnp.dot(
                 xt[...], g, preferred_element_type=jnp.float32
             ).astype(jnp.bfloat16)
-        dw_store(t, base).start()
 
     def dwp_copy(t, base):
         k = t - BEFORE
-        return remote(dwp.at[k], dw_hbm.at[:, pl.ds(base, pair)], dwp_send.at[k], dwp_recv.at[k], far_dev)
+        return remote(dwp.at[k], dw_ref.at[:, pl.ds(base, pair)], dwp_send.at[k], dwp_recv.at[k], far_dev)
 
     def dwp_part(t):
         for chunk in range(2):
@@ -229,6 +243,8 @@
 
             @pl.when(jnp.logical_and(t >= 0, t < ticks))
             def _(t=t, stage=stage):
+                if stage == 1:
+                    arrive(t, 4)
                 arrive(t, stage - 1)
                 start(t, stage)
 
@@ -239,9 +255,11 @@
     lax.fori_loop(0, LEAD[0] + LAG, fill, 0)
 
     x_in[0].wait_recv()
-    x_out[4].start()
+    x_out[5].start()
     x_in[1].wait_recv()
-    x_in[4].wait_recv()
+    x_out[6].start()
+    x_in[2].wait_recv()
+    x_in[5].wait_recv()
     load_w.wait()
 
     def tick(place, t, carry):
@@ -273,23 +291,23 @@
 
     lax.fori_loop(0, BEFORE, functools.partial(tick, early), 0)
 
-    for k in (2, 3):
-        x_in[k].wait_recv()
-        x_out[k + 3].start()
-    x_in[5].wait_recv()
+    x_in[3].wait_recv()
+    x_in[4].wait_recv()
+    x_out[7].start()
     x_in[6].wait_recv()
+    x_in[7].wait_recv()
 
     lax.fori_loop(BEFORE, after, paired_tick, 0)
 
     give = []
-    for k, s in enumerate((1 - side, side)):
+    for k, s in enumerate((side, 1 - side)):
         copy = remote(accp.at[s * 2 + 1 - core], from_core_p.at[k], r_send.at[k], r_recv.at[k], core_dev)
         copy.start()
         give.append(copy)
-    for k, (s, dev) in enumerate(((1 - side, diag_dev), (side, far_dev))):
+    for k, s in enumerate((side, 1 - side)):
         give[k].wait_recv()
         to_chips[k] = (accp[s * 2 + core] + from_core_p[k]).astype(jnp.bfloat16)
-        copy = remote(to_chips.at[k], from_chips.at[k], r_send.at[2 + k], r_recv.at[2 + k], dev)
+        copy = remote(to_chips.at[k], from_chips.at[k], r_send.at[2 + k], r_recv.at[2 + k], diag_dev)
         copy.start()
         give.append(copy)
 
@@ -299,39 +317,63 @@
     advance(last + LAG)
     arrive(last, 3)
 
-    def owner_of(s, c):
-        return s * 2 + c
-
-    for k, s in enumerate((1 - side, side)):
-        j = owner_of(s, 1 - core)
-        dx_part(last, late(last), j)
-        copy = remote(acc.at[j], from_core.at[k], r_send.at[4 + k], r_recv.at[4 + k], core_dev)
+    half = rows // 2
+
+    def dx_half(owner, h):
+        total = acc[owner, h * half : (h + 1) * half]
+        for chunk in range(2):
+            cols = pl.ds(pl.multiple_of(late(last) + chunk * WIDTH, WIDTH), WIDTH)
+            g = gall[last, chunk, owner, h].reshape(half, WIDTH)
+            total += lax.dot_general(g, wv[:, cols], (((1,), (1,)), ((), ())), preferred_element_type=jnp.float32)
+        return total
+
+    def part(h):
+        return pl.ds(h * half, half)
+
+    def exchange(k, src, dst, dev):
+        copy = remote(src, dst, r_send.at[k], r_recv.at[k], dev)
         copy.start()
         give.append(copy)
-    dx_part(last, late(last), owner_of(1 - side, core))
-    give[4].wait_recv()
-    to_chips[2] = (acc[owner_of(1 - side, core)] + from_core[0]).astype(jnp.bfloat16)
-    across = remote(to_chips.at[2], from_chips.at[2], r_send.at[6], r_recv.at[6], side_dev)
-    across.start()
-    give.append(across)
-    dx_part(last, late(last), owner_of(side, core))
+        return copy
+
+    to_core = []
+    for h in range(2):
+        j = (1 - side) * 2 + 1 - core
+        acc[j, h * half : (h + 1) * half] = dx_half(j, h)
+        to_core.append(exchange(4 + h, acc.at[j, part(h)], from_core.at[0, part(h)], core_dev))
+    across = []
+    for h in range(2):
+        total = dx_half((1 - side) * 2 + core, h)
+        to_core[h].wait_recv()
+        if h == 0:
+            give[2].wait_recv()
+        total += from_core[0, h * half : (h + 1) * half]
+        total += from_chips[0, h * half : (h + 1) * half].astype(jnp.float32)
+        to_chips[2, h * half : (h + 1) * half] = total.astype(jnp.bfloat16)
+        across.append(exchange(6 + h, to_chips.at[2, part(h)], from_chips.at[2, part(h)], side_dev))
+    for h in range(2):
+        j = side * 2 + 1 - core
+        acc[j, h * half : (h + 1) * half] = dx_half(j, h)
+        to_core.append(exchange(8 + h, acc.at[j, part(h)], from_core.at[1, part(h)], core_dev))
     dw_part(last, late(last))
-    give[5].wait_recv()
-    give[2].wait_recv()
-    give[3].wait_recv()
-    total = acc[owner_of(side, core)] + from_core[1]
-    total += from_chips[0].astype(jnp.float32) + from_chips[1].astype(jnp.float32)
-    across.wait_recv()
-    dx_ref[...] = (total + from_chips[2].astype(jnp.float32)).astype(jnp.bfloat16)
+    for h in range(2):
+        j = side * 2 + core
+        total = dx_half(j, h)
+        to_core[2 + h].wait_recv()
+        acc[j, h * half : (h + 1) * half] = total + from_core[1, h * half : (h + 1) * half]
+    for h in range(2):
+        total = acc[side * 2 + core, h * half : (h + 1) * half]
+        if h == 0:
+            give[3].wait_recv()
+        total += from_chips[1, h * half : (h + 1) * half].astype(jnp.float32)
+        across[h].wait_recv()
+        other = from_chips[2, h * half : (h + 1) * half].astype(jnp.float32)
+        dx_ref[h * half : (h + 1) * half, :] = (total + other).astype(jnp.bfloat16)
 
     def finish(t, carry):
         far_in(t).wait_send()
-        for stage in range(4):
+        for stage in range(5):
             sent(t, stage)
-        return carry
-
-    def stored(place, t, carry):
-        dw_store(t, place(t)).wait()
         return carry
 
     def exchanged(t, carry):
@@ -340,9 +382,6 @@
         return carry
 
     lax.fori_loop(0, ticks, finish, 0)
-    lax.fori_loop(0, BEFORE, functools.partial(stored, early), 0)
-    lax.fori_loop(BEFORE, after, functools.partial(stored, mine), 0)
-    lax.fori_loop(after, ticks, functools.partial(stored, late), 0)
     lax.fori_loop(BEFORE, after, exchanged, 0)
     for copy in x_out:
         copy.wait_send()
@@ -362,10 +401,10 @@
         functools.partial(kernel, ticks),
         out_shape=(
             jax.ShapeDtypeStruct((rows, model), jnp.bfloat16),
-            jax.ShapeDtypeStruct((model, hidden), jnp.bfloat16),
+            pltpu.VMEM((model, hidden), jnp.bfloat16),
         ),
         in_specs=[vmem, vmem, vmem, hbm],
-        out_specs=(vmem, hbm),
+        out_specs=(vmem, vmem),
         scratch_shapes=[
             pltpu.VMEM((ticks, 2, 4, 2, 4, tokens, WIDTH), jnp.bfloat16),
             pltpu.VMEM((PAIRED, 2, tokens, WIDTH), jnp.bfloat16),
@@ -375,29 +414,27 @@
             pltpu.VMEM((model, 4 * rows), jnp.bfloat16),
             pltpu.VMEM((4, rows, model), jnp.float32),
             pltpu.VMEM((4, rows, model), jnp.float32),
-            pltpu.VMEM((ticks, model, pair), jnp.bfloat16),
             pltpu.VMEM((PAIRED, model, pair), jnp.bfloat16),
             pltpu.VMEM((2, rows, model), jnp.float32),
             pltpu.VMEM((2, rows, model), jnp.float32),
             pltpu.VMEM((3, rows, model), jnp.bfloat16),
             pltpu.VMEM((3, rows, model), jnp.bfloat16),
-            dma((ticks, 4, 2, 2)),
-            dma((ticks, 4, 2, 2)),
+            dma((ticks, 5, 2, 2)),
+            dma((ticks, 5, 2, 2)),
             dma((ticks,)),
             dma((ticks,)),
-            dma((7,)),
-            dma((7,)),
-            dma((7,)),
-            dma((7,)),
+            dma((8,)),
+            dma((8,)),
+            dma((11,)),
+            dma((11,)),
             dma((PAIRED,)),
             dma((PAIRED,)),
             dma((PAIRED,)),
             dma((PAIRED,)),
             dma,
-            dma((ticks,)),
         ],
         compiler_params=pltpu.CompilerParams(
-            collective_id=0, has_side_effects=True, vmem_limit_bytes=60 * 2**20
+            collective_id=0, has_side_effects=True, vmem_limit_bytes=48 * 2**20
         ),
         name="gather_and_multiply",
     )(inputs, saved_pre, grad_hidden, weight_in)

time: 136 us -> 128 us (0.941)
  Pallas kernels: 129 us -> 123 us
  local copies, waits for them, and re-layouts: 6.83 us -> 3.92 us
    pallas_call x1, Pallas kernels: 129 us -> 123 us  [local(): pl.pallas_call(functools.partial(kernel, ticks), out_shape=(jax.ShapeDtyp...]
    unnamed x2 -> x4, local copies, waits for them, and re-layouts: 6.83 us -> 3.92 us
where the time goes in v3:
time: 128 us; the launch traced here: 127 us
  Pallas kernels  123 us (96%)
  local copies, waits for them, and re-layouts  3.92 us (3%)
    pallas_call x1, Pallas kernels, local(): pl.pallas_call(functools.partial(kernel, ticks), out_shape=(jax.ShapeDtyp...  123 us
    unnamed x4, local copies, waits for them, and re-layouts  3.92 us

profile of v3, /device:TPU:1, one launch (start us, length us, event | category | flops | bytes accessed | tf_op | source)
XLA Modules:
  0.0 127.2 jit_solution(1074446682966399126)
XLA Ops:
  0.6 0.0 copy-start
  0.6 1.0 copy-done
  1.6 122.6 %gather_and_multiply.1 = (bf16[512,384]{1,0:T(8,128)(2,1)S(1)}, bf16[384,6144]{1,0:T(8,128)(2,1)S(1)}) custom-call(bf16[512,384]{1,0:T(8,128)(2,1)S(1)} %copy-done, bf16[64,6144]{1,0:T(8,128)(2,1)} %pre_ref.1, bf16[64,6144]{1,0:T(8,128)(2,1)} %gh_ref.1, bf16[384,6144]{1,0:T(8,128)(2,1)} %w_hbm.1), custom_call_target="tpu_custom_call" | custom-call | tf_op jit(solution)/shard_map/gather_and_multiply/pallas_call | solution.py:400
  124.2 2.2 %copy.8 = bf16[384,6144]{1,0:T(8,128)(2,1)} copy(bf16[384,6144]{1,0:T(8,128)(2,1)S(1)} %get-tuple-element.3) | data formatting | bytes 9437184
  126.4 0.7 copy.9
Async XLA Ops:
  0.6 1.0 copy-start

commit v4 on v3

--- a/solution.py
+++ b/solution.py
@@ -11,7 +11,7 @@
 WIDTH = 256
 LEAD = (3, 2, 1, 0)
 LAG = 1
-PAIRED = 3
+PAIRED = 4
 BEFORE = 1
 ROOT = 0.7978845608028654
 CUBE = 0.044715
@@ -25,9 +25,9 @@
     return (grad_hidden.astype(jnp.float32) * slope).astype(jnp.bfloat16)
 
 
-def kernel(ticks, x_ref, pre_ref, gh_ref, w_hbm, dx_ref, dw_ref, gall, gout, wv, wp, xt, xtp, acc, accp, dwp,
-           from_core, from_core_p, to_chips, from_chips, g_send, g_recv, p_send, p_recv, x_send, x_recv, r_send, r_recv,
-           wp_send, wp_recv, dwp_send, dwp_recv, w_sem):
+def kernel(ticks, x_hbm, pre_hbm, gh_hbm, w_hbm, dx_ref, dw_ref, gall, gout, wv, wp, xt, xtp, acc, accp, dwp,
+           x_ref, pre_ref, gh_ref, from_core, from_core_p, to_chips, from_chips, g_send, g_recv, p_send, p_recv, x_send, x_recv, r_send, r_recv,
+           wp_send, wp_recv, dwp_send, dwp_recv, w_sem, in_sem):
     y = lax.axis_index("row")
     col = lax.axis_index("col")
     depth = lax.axis_index("depth")
@@ -45,6 +45,12 @@
     pair = 2 * WIDTH
 
     load_w = pltpu.make_async_copy(w_hbm, wv, w_sem)
+    loads = [
+        pltpu.make_async_copy(src, dst, in_sem.at[k])
+        for k, (src, dst) in enumerate(((pre_hbm, pre_ref), (gh_hbm, gh_ref), (x_hbm, x_ref)))
+    ]
+    for copy in loads:
+        copy.start()
     load_w.start()
 
     barrier = pltpu.get_barrier_semaphore()
@@ -128,10 +134,13 @@
         return carry
 
     after = BEFORE + PAIRED
+    loads[0].wait()
+    loads[1].wait()
     lax.fori_loop(0, BEFORE, functools.partial(own_grad, early), 0)
     lax.fori_loop(BEFORE, after, paired_grad, 0)
     lax.fori_loop(after, ticks, functools.partial(own_grad, late), 0)
     own = pl.ds(pl.multiple_of(col * rows, rows), rows)
+    loads[2].wait()
     xt[:, own] = x_ref[...].T
     pl.semaphore_wait(barrier, 8)
 
@@ -162,8 +171,8 @@
         x_copy(0, xt.at[:, own], xt.at[:, own], side_dev),
         x_copy(1, xt.at[:, own], xtp.at[:, own], diag_dev),
         x_copy(2, xt.at[:, own], xt.at[:, own], core_dev),
-        x_copy(3, xt.at[low, own], xtp.at[low, own], far_dev),
-        x_copy(4, xt.at[high, own], xtp.at[high, own], far_dev),
+        x_copy(3, xt.at[low, beside], xtp.at[low, beside], diag_dev),
+        x_copy(4, xtp.at[high, beside], xtp.at[high, beside], side_dev),
         x_copy(5, xt.at[:, beside], xt.at[:, beside], core_dev),
         x_copy(6, xtp.at[:, beside], xtp.at[:, beside], core_dev),
         x_copy(7, xtp.at[:, own], xtp.at[:, own], core_dev),
@@ -178,7 +187,7 @@
         x_copy(6, xtp.at[:, cross], xtp.at[:, cross], core_dev),
         x_copy(7, xtp.at[:, near], xtp.at[:, near], core_dev),
     ]
-    for copy in x_out[:5]:
+    for copy in x_out[:3]:
         copy.start()
     lax.fori_loop(after, ticks, own_out, 0)
 
@@ -191,7 +200,7 @@
         wp_copy(k).start()
         return carry
 
-    lax.fori_loop(0, PAIRED, send_weights, 0)
+    lax.fori_loop(0, 1, send_weights, 0)
 
     accp[...] = jnp.zeros_like(accp)
     acc[...] = jnp.zeros_like(acc)
@@ -255,8 +264,11 @@
     lax.fori_loop(0, LEAD[0] + LAG, fill, 0)
 
     x_in[0].wait_recv()
+    x_out[3].start()
+    x_in[1].wait_recv()
+    x_out[4].start()
+    lax.fori_loop(1, PAIRED, send_weights, 0)
     x_out[5].start()
-    x_in[1].wait_recv()
     x_out[6].start()
     x_in[2].wait_recv()
     x_in[5].wait_recv()
@@ -400,10 +412,10 @@
     return pl.pallas_call(
         functools.partial(kernel, ticks),
         out_shape=(
-            jax.ShapeDtypeStruct((rows, model), jnp.bfloat16),
+            pltpu.VMEM((rows, model), jnp.bfloat16),
             pltpu.VMEM((model, hidden), jnp.bfloat16),
         ),
-        in_specs=[vmem, vmem, vmem, hbm],
+        in_specs=[hbm, hbm, hbm, hbm],
         out_specs=(vmem, vmem),
         scratch_shapes=[
             pltpu.VMEM((ticks, 2, 4, 2, 4, tokens, WIDTH), jnp.bfloat16),
@@ -415,6 +427,9 @@
             pltpu.VMEM((4, rows, model), jnp.float32),
             pltpu.VMEM((4, rows, model), jnp.float32),
             pltpu.VMEM((PAIRED, model, pair), jnp.bfloat16),
+            pltpu.VMEM((rows, model), jnp.bfloat16),
+            pltpu.VMEM((tokens, hidden), jnp.bfloat16),
+            pltpu.VMEM((tokens, hidden), jnp.bfloat16),
             pltpu.VMEM((2, rows, model), jnp.float32),
             pltpu.VMEM((2, rows, model), jnp.float32),
             pltpu.VMEM((3, rows, model), jnp.bfloat16),
@@ -432,9 +447,10 @@
             dma((PAIRED,)),
             dma((PAIRED,)),
             dma,
+            dma((3,)),
         ],
         compiler_params=pltpu.CompilerParams(
-            collective_id=0, has_side_effects=True, vmem_limit_bytes=48 * 2**20
+            collective_id=0, has_side_effects=True, vmem_limit_bytes=50 * 2**20
         ),
         name="gather_and_multiply",
     )(inputs, saved_pre, grad_hidden, weight_in)

time: 128 us -> 125 us (0.977)
    unnamed x4 -> x2, local copies, waits for them, and re-layouts: 3.92 us -> 2.93 us
where the time goes in v4:
time: 125 us
  Pallas kernels  122 us (98%)
  local copies, waits for them, and re-layouts  2.93 us (2%)
    pallas_call x1, Pallas kernels, local(): pl.pallas_call(functools.partial(kernel, ticks), out_shape=(pltpu.VMEM((r...  122 us
    unnamed x2, local copies, waits for them, and re-layouts  2.93 us

profile of v4, /device:TPU:1, one launch (start us, length us, event | category | flops | bytes accessed | tf_op | source)
XLA Modules:
  0.0 125.4 jit_solution(11853578659411163257)
XLA Ops:
  0.6 121.8 %gather_and_multiply.1 = (bf16[512,384]{1,0:T(8,128)(2,1)S(1)}, bf16[384,6144]{1,0:T(8,128)(2,1)S(1)}) custom-call(bf16[512,384]{1,0:T(8,128)(2,1)} %x_hbm.1, bf16[64,6144]{1,0:T(8,128)(2,1)} %pre_hbm.1, bf16[64,6144]{1,0:T(8,128)(2,1)} %gh_hbm.1, bf16[384,6144]{1,0:T(8,128)(2,1)} %w_hbm.1), custom_call_target="tpu_custom_call" | custom-call | tf_op jit(solution)/shard_map/gather_and_multiply/pallas_call | solution.py:412
  122.5 0.7 copy.8
  123.2 2.2 %copy.9 = bf16[384,6144]{1,0:T(8,128)(2,1)} copy(bf16[384,6144]{1,0:T(8,128)(2,1)S(1)} %get-tuple-element.3) | data formatting | bytes 9437184
